TPU v7x, 32 devices: a whole 2x2x4 slice. The times are simulated.
32 devices in a mesh: group: 2 (over y), lender: 4 (over z), tensor: 4 (over x, core).
Axes of the slice: x: 2, y: 2, z: 4, core: 2. Of those that a mesh axis runs over, the one named last changes fastest.
Arguments:
- activations: bfloat16 [16, 8192], P('group', 'lender'), parts along dimension 0, may hold values from -400 to 400
- norm_gain: bfloat16 [8192], P('lender'), may hold values from 0.099609375 to 1.8984375
- w_query: bfloat16 [8192, 8192], P('lender', 'tensor'), may hold values from -0.0625 to 0.0625
- w_out: bfloat16 [8192, 8192], P('tensor', 'lender'), may hold values from -0.0625 to 0.0625
- key_pool: bfloat16 [8, 256, 128, 128], P('tensor', ('group', 'lender')), parts along dimension 1, may hold values from -800 to 800
- value_block_store: bfloat16 [8, 256, 128, 128], P('tensor', ('group', 'lender')), parts along dimension 1, may hold values from -48 to 48
- block_list: int32 [16, 8, 16], P('group', 'tensor'), parts along dimension 0, may hold values from 0 to 127, as said below
- block_slot_table: int32 [8, 256], P('tensor', 'group'), parts along dimension 1, may hold values from 0 to 127, each once within a row
- kept_len: int32 [16, 8], P('group', 'tensor'), parts along dimension 0, may hold values from 1 to 16, as said below
Outputs:
- output: bfloat16 [16, 8192], P(('group', 'tensor'), 'lender'), parts along dimension 0
There are 2 independent parts, one for each index of `group`. A program takes and returns all parts, laid end to end along the dimension named above; an argument that names none is the same for every part. Nothing has to cross between parts.
Inputs may be any that keep to these rules, and one draw needn't show every extreme that they name: `block_list`: for each KV head, no logical block appears twice among all rows' lists. `kept_len`: some row of every KV head keeps 16 blocks and some other row keeps one.
All inputs are finite; a program needn't handle non-finite values.
Results may differ from a plain program's by a relative error of at most 0.012.
The roundings to bfloat16 on the way count: a program that leaves them out, or rounds other values in their place, can miss the bound.
Values may be sent and summed in bfloat16 or wider, within the bound.
A program may use at most 64 MiB of HBM per device.

v0:
```python
import functools

import jax
import jax.numpy as jnp
from jax import lax
from jax.experimental import pallas as pl
from jax.experimental.pallas import tpu as pltpu
from jax.sharding import PartitionSpec as P

very_low = -1e30
epsilon = 1e-05


def separate_ops(
    activations,
    norm_gain,
    w_query,
    w_out,
    key_pool,
    value_block_store,
    block_list,
    block_slot_table,
    kept_len,
):
    row_count = activations.shape[0]
    kv_heads = key_pool.shape[0]
    slot_count = key_pool.shape[1]
    head_dim = key_pool.shape[3]
    kept_most = block_list.shape[2]
    features = activations.astype(jnp.float32)
    squares = jnp.sum(features * features, axis=1)
    scaled = (features * norm_gain.astype(jnp.float32)).astype(jnp.bfloat16)
    partial_value = jnp.dot(scaled, w_query, preferred_element_type=jnp.float32)
    projected, square_sum = lax.psum((partial_value, squares), "lender")
    width = features.shape[1] * lax.axis_size("lender")
    inverse = lax.rsqrt(square_sum / width + epsilon)
    query_vectors = (projected * inverse[:, None] * head_dim ** (-0.5)).astype(jnp.bfloat16)
    group_size = query_vectors.shape[1] // (kv_heads * head_dim)
    query_vectors = query_vectors.reshape(row_count, kv_heads, group_size, head_dim)
    slot_lookup_table = jnp.broadcast_to(
        block_slot_table[None], (row_count,) + block_slot_table.shape
    )
    slot_ids = jnp.take_along_axis(slot_lookup_table, block_list, axis=2)
    positions = jnp.arange(kept_most, dtype=jnp.int32)
    is_live = positions[None, None, :] < kept_len[:, :, None]
    local_slot = slot_ids - lax.axis_index("lender") * slot_count
    matches = is_live[..., None] & (
        local_slot[..., None] == jnp.arange(slot_count, dtype=jnp.int32)
    )
    owner_mask = jnp.transpose(jnp.any(matches, axis=2), (1, 2, 0))
    owner_half = owner_mask.astype(jnp.bfloat16)
    owner_full = owner_mask.astype(jnp.float32)
    used_slot = jnp.any(owner_mask, axis=2)
    picked = jnp.einsum(
        "hsr,rhgd->hsgd", owner_half, query_vectors, preferred_element_type=jnp.float32
    ).astype(jnp.bfloat16)
    scores = jnp.einsum("hsgd,hstd->hsgt", picked, key_pool, preferred_element_type=jnp.float32)
    block_best = jnp.max(scores, axis=3)
    spread = jnp.where(owner_mask[..., None], block_best[:, :, None, :], very_low)
    row_best = jnp.max(spread, axis=1)
    slot_best = jnp.max(jnp.where(owner_mask[..., None], row_best[:, None, :, :], very_low), axis=2)
    slot_best = jnp.where(used_slot[..., None], slot_best, 0.0)
    weights_full = jnp.where(
        used_slot[:, :, None, None], jnp.exp(scores - slot_best[..., None]), 0.0
    )
    slot_weight = jnp.sum(weights_full, axis=3)
    slot_value = jnp.einsum(
        "hsgt,hstd->hsgd",
        weights_full.astype(jnp.bfloat16),
        value_block_store,
        preferred_element_type=jnp.float32,
    )
    row_weight = jnp.einsum(
        "hsr,hsg->rhg", owner_full, slot_weight, precision=lax.Precision.HIGHEST
    )
    row_value = jnp.einsum(
        "hsr,hsgd->rhgd", owner_full, slot_value, precision=lax.Precision.HIGHEST
    )
    row_high = jnp.transpose(row_best, (1, 0, 2))
    lenders = lax.axis_size("lender")
    home_rows = row_count // lenders
    came_best, came_weight, came_value = (
        lax.all_to_all(row_high, "lender", split_axis=0, concat_axis=0, tiled=True),
        lax.all_to_all(row_weight, "lender", split_axis=0, concat_axis=0, tiled=True),
        lax.all_to_all(row_value, "lender", split_axis=0, concat_axis=0, tiled=True),
    )
    came_best = came_best.reshape((lenders, home_rows) + came_best.shape[1:])
    came_weight = came_weight.reshape((lenders, home_rows) + came_weight.shape[1:])
    came_value = came_value.reshape((lenders, home_rows) + came_value.shape[1:])
    highest = jnp.max(came_best, axis=0)
    factor = jnp.exp(came_best - highest[None])
    home_weight = jnp.sum(came_weight * factor, axis=0)
    home_value = jnp.sum(came_value * factor[..., None], axis=0)
    home_attended = (
        (home_value / home_weight[..., None]).astype(jnp.bfloat16).reshape(home_rows, -1)
    )
    attended = lax.all_gather(home_attended, "lender", axis=0, tiled=True)
    result = lax.psum_scatter(
        jnp.dot(attended, w_out, preferred_element_type=jnp.float32),
        "tensor",
        scatter_dimension=0,
        tiled=True,
    )
    return result.astype(jnp.bfloat16)


MESH = pl.DeviceIdType.MESH
LANES = 128
SUBLANES = 8


def fused_kernel(
    lenders,
    tensors,
    act_hbm,
    gain_hbm,
    list_hbm,
    table_hbm,
    kept_hbm,
    wq_hbm,
    wo_hbm,
    key_hbm,
    value_hbm,
    out_ref,
    act_ref,
    gain_ref,
    list_ref,
    table_ref,
    kept_ref,
    wq,
    wo,
    keys,
    values,
    q_send,
    q_recv,
    q_all,
    bias,
    scores,
    part_send,
    part_recv,
    att_all,
    sum_send,
    sum_recv,
    small_sem,
    wq_sem,
    wo_sem,
    kv_sem,
    lender_send,
    lender_recv,
    tensor_send,
    tensor_recv,
):
    me = lax.axis_index("lender")
    mine = lax.axis_index("tensor")
    rows = act_ref.shape[0]
    kv_heads, slot_count, tokens, head_dim = keys.shape
    width = wq.shape[2]
    chunk_heads = width // head_dim
    chunk_rows = chunk_heads * rows
    group = wo.shape[0] * chunk_heads // kv_heads
    chunks_per_kv = group // chunk_heads
    kept_most = list_ref.shape[2]
    f32, bf16 = jnp.float32, jnp.bfloat16

    def lender_at(offset):
        return lax.rem(me + offset, lenders)

    far_first = sorted(range(1, lenders), key=lambda offset: abs(2 * offset - lenders))
    small_copies = [
        pltpu.make_async_copy(src, dst, small_sem.at[at])
        for at, (src, dst) in enumerate(
            (
                (act_hbm, act_ref),
                (gain_hbm, gain_ref),
                (list_hbm, list_ref),
                (table_hbm, table_ref),
                (kept_hbm, kept_ref),
            )
        )
    ]
    wq_copies = []
    for offset in far_first + [0]:
        columns = pl.ds(pl.multiple_of(lender_at(offset) * width, width), width)
        wq_copies.append(
            pltpu.make_async_copy(wq_hbm.at[:, columns], wq.at[offset], wq_sem.at[offset])
        )
    key_copy = pltpu.make_async_copy(key_hbm, keys, kv_sem.at[0])
    value_copy = pltpu.make_async_copy(value_hbm, values, kv_sem.at[1])
    wo_copies = []
    for offset in range(lenders):
        source = lender_at(lenders - offset)
        lines = pl.ds(pl.multiple_of(source * width, width), width)
        wo_copies.append(
            pltpu.make_async_copy(wo_hbm.at[lines], wo.at[offset], wo_sem.at[offset])
        )
    for copy in small_copies[:2]:
        copy.start()
    for copy in wq_copies:
        copy.start()

    barrier = pltpu.get_barrier_semaphore()
    for offset in range(1, lenders):
        pl.semaphore_signal(
            barrier, inc=1, device_id={"lender": lender_at(offset)}, device_id_type=MESH
        )
    for offset in range(1, tensors):
        pl.semaphore_signal(
            barrier,
            inc=1,
            device_id={"tensor": lax.rem(mine + offset, tensors)},
            device_id_type=MESH,
        )

    def to_lender(stage, offset, src, dst):
        return pltpu.make_async_remote_copy(
            src_ref=src,
            dst_ref=dst,
            send_sem=lender_send.at[stage, offset],
            recv_sem=lender_recv.at[stage, offset],
            device_id={"lender": lender_at(offset)},
            device_id_type=MESH,
        )

    for copy in small_copies[:2]:
        copy.wait()
    features = act_ref[...].astype(f32)
    squares = jnp.sum(features * features, axis=1, keepdims=True)
    scaled = (features * gain_ref[...].astype(f32).reshape(1, -1)).astype(bf16)

    started = []
    own_partial = None
    for at, offset in enumerate(far_first + [0]):
        wq_copies[at].wait()
        if at == 0:
            for copy in small_copies[2:]:
                copy.start()
            key_copy.start()
            value_copy.start()
        if at == min(1, lenders - 1):
            for copy in wo_copies:
                copy.start()
        partial = jnp.dot(scaled, wq[offset], preferred_element_type=f32)
        if offset == 0:
            own_partial = partial
            continue
        q_send[offset, :, :width] = partial
        q_send[offset, :, width:] = jnp.broadcast_to(squares, (rows, LANES))
        if at == 0:
            pl.semaphore_wait(barrier, lenders + tensors - 2)
        copy = to_lender(0, offset, q_send.at[offset], q_recv.at[offset])
        copy.start()
        started.append(copy)

    for copy in small_copies[2:]:
        copy.wait()
    blocks = table_ref.shape[1]
    block_ids = lax.broadcasted_iota(jnp.int32, (rows, blocks), 1)
    local_slots = lax.broadcasted_iota(jnp.int32, (slot_count, blocks), 0) + me * slot_count
    row_eye = lax.broadcasted_iota(jnp.int32, (rows, rows), 0) == lax.broadcasted_iota(
        jnp.int32, (rows, rows), 1
    )
    for h in range(kv_heads):
        member = jnp.zeros((rows, blocks), f32)
        listed = list_ref[:, h, :]
        kept = jnp.sum(jnp.where(row_eye, kept_ref[h : h + 1, :], 0), axis=1, keepdims=True)
        for k in range(kept_most):
            hit = (listed[:, k : k + 1] == block_ids) & (kept > k)
            member = jnp.where(hit, 1.0, member)
        holds = jnp.where(table_ref[h : h + 1, :] == local_slots, 1.0, 0.0)
        owner = lax.dot_general(
            member.astype(bf16),
            holds.astype(bf16),
            (((1,), (1,)), ((), ())),
            preferred_element_type=f32,
        )
        lowered = (owner - 1.0) * -very_low
        for s in range(slot_count):
            bias[h, :, s * tokens : (s + 1) * tokens] = jnp.broadcast_to(
                lowered[:, s : s + 1], (rows, tokens)
            )

    projected, square_sum = own_partial, squares
    for copy in started:
        copy.wait_recv()
    for offset in range(1, lenders):
        projected = projected + q_recv[offset, :, :width]
        square_sum = square_sum + q_recv[offset, :, width : width + 1]
    inverse = lax.rsqrt(square_sum / (act_ref.shape[1] * lenders) + epsilon)
    normed = projected * inverse * head_dim ** (-0.5)
    q_all[me] = jnp.concatenate(
        [normed[:, j * head_dim : (j + 1) * head_dim] for j in range(chunk_heads)], axis=0
    ).astype(bf16)
    for offset in far_first:
        copy = to_lender(1, offset, q_all.at[me], q_all.at[me])
        copy.start()
        started.append(copy)

    step_slots = max(1, min(slot_count, 512 // tokens))
    step = step_slots * tokens
    steps = slot_count // step_slots
    eye = lax.broadcasted_iota(jnp.int32, (chunk_rows, LANES), 0) == lax.broadcasted_iota(
        jnp.int32, (chunk_rows, LANES), 1
    )
    first_line = lax.broadcasted_iota(jnp.int32, (SUBLANES, LANES), 0) == 0
    for h in range(kv_heads):
        chunks = range(h * chunks_per_kv, (h + 1) * chunks_per_kv)
        for source in chunks:

            @pl.when(me != source)
            def _():
                offset = lax.rem(me - source + lenders, lenders)
                to_lender(1, offset, q_all.at[source], q_all.at[source]).wait_recv()

        if h == 0:
            key_copy.wait()
        queries = q_all[chunks.start : chunks.stop].reshape(group * rows, head_dim)
        running = None
        for c in range(steps):
            block = keys[h, c * step_slots : (c + 1) * step_slots].reshape(step, head_dim)
            found = lax.dot_general(
                queries, block, (((1,), (1,)), ((), ())), preferred_element_type=f32
            )
            found = found.reshape(group, rows, step) + bias[h, :, c * step : (c + 1) * step][None]
            found = found.reshape(group * rows, step)
            scores[h, :, c * step : (c + 1) * step] = found
            for t in range(0, step, LANES):
                piece = found[:, t : t + LANES]
                running = piece if running is None else jnp.maximum(running, piece)
        best = jnp.max(running, axis=1, keepdims=True)
        if h == 0:
            value_copy.wait()
        total = None
        gathered = jnp.zeros((group * rows, head_dim), f32)
        for c in range(steps):
            weights = jnp.exp(scores[h, :, c * step : (c + 1) * step] - best)
            for t in range(0, step, LANES):
                piece = weights[:, t : t + LANES]
                total = piece if total is None else total + piece
            block = values[h, c * step_slots : (c + 1) * step_slots].reshape(step, head_dim)
            gathered = gathered + jnp.dot(
                weights.astype(bf16), block, preferred_element_type=f32
            )
        total = jnp.sum(total, axis=1, keepdims=True)
        for j, d in enumerate(chunks):
            lines = slice(j * chunk_rows, (j + 1) * chunk_rows)
            best_line = jnp.sum(jnp.where(eye, best[lines], 0.0), axis=0, keepdims=True)
            total_line = jnp.sum(jnp.where(eye, total[lines], 0.0), axis=0, keepdims=True)
            part_send[d, :chunk_rows, :] = gathered[lines]
            part_send[d, chunk_rows:, :] = jnp.where(first_line, best_line, total_line)
        for d in chunks:

            @pl.when(me != d)
            def _():
                offset = lax.rem(d - me + lenders, lenders)
                to_lender(2, offset, part_send.at[d], part_recv.at[offset]).start()

    part_recv[0] = part_send[me]
    for offset in range(1, lenders):
        copy = to_lender(2, offset, part_send.at[lender_at(offset)], part_recv.at[offset])
        copy.wait_recv()
        started.append(copy)
    bests, totals = [], []
    for offset in range(lenders):
        line = part_recv[offset, chunk_rows : chunk_rows + 1, :]
        bests.append(jnp.sum(jnp.where(eye, line, 0.0), axis=1, keepdims=True))
        line = part_recv[offset, chunk_rows + 1 : chunk_rows + 2, :]
        totals.append(jnp.sum(jnp.where(eye, line, 0.0), axis=1, keepdims=True))
    highest = functools.reduce(jnp.maximum, bests)
    home_total = jnp.zeros((chunk_rows, 1), f32)
    home_value = jnp.zeros((chunk_rows, head_dim), f32)
    for offset in range(lenders):
        factor = jnp.exp(bests[offset] - highest)
        home_total = home_total + totals[offset] * factor
        home_value = home_value + part_recv[offset, :chunk_rows, :] * factor
    att_all[me] = (home_value / home_total).astype(bf16)
    att_copies = {}
    for offset in far_first:
        copy = to_lender(3, offset, att_all.at[me], att_all.at[me])
        copy.start()
        att_copies[offset] = copy
    started += att_copies.values()

    product = None
    for offset in range(lenders):
        wo_copies[offset].wait()
        if offset > 0:
            att_copies[offset].wait_recv()
        chunk = att_all[lender_at(lenders - offset)].astype(f32)
        chunk = jnp.concatenate(
            [chunk[j * rows : (j + 1) * rows] for j in range(chunk_heads)], axis=1
        ).astype(bf16)
        term = jnp.dot(chunk, wo[offset], preferred_element_type=f32)
        product = term if product is None else product + term

    home_rows = rows // tensors
    part_width = product.shape[1] // tensors
    line_block = lax.broadcasted_iota(jnp.int32, (rows, part_width), 0) // home_rows
    for d in range(tensors):
        packed = jnp.zeros((rows, part_width), f32)
        for c in range(tensors):
            piece = product[:, c * part_width : (c + 1) * part_width]
            shift = (c - d) * home_rows % rows
            if shift:
                piece = pltpu.roll(piece, shift, 0)
            packed = jnp.where(line_block == c, piece, packed)
        sum_send[d] = packed
    for offset in range(1, tensors):
        target = lax.rem(mine + offset, tensors)
        copy = pltpu.make_async_remote_copy(
            src_ref=sum_send.at[target],
            dst_ref=sum_recv.at[offset],
            send_sem=tensor_send.at[offset],
            recv_sem=tensor_recv.at[offset],
            device_id={"tensor": target},
            device_id_type=MESH,
        )
        copy.start()
        started.append(copy)
    result = sum_send[mine]
    for copy in started[1 - tensors :] if tensors > 1 else []:
        copy.wait_recv()
    for offset in range(1, tensors):
        result = result + sum_recv[offset]
    for c in range(tensors):
        out_ref[:, c * part_width : (c + 1) * part_width] = result[
            c * home_rows : (c + 1) * home_rows
        ].astype(out_ref.dtype)
    for copy in started:
        copy.wait_send()


def fused(
    activations,
    norm_gain,
    w_query,
    w_out,
    key_pool,
    value_block_store,
    block_list,
    block_slot_table,
    kept_len,
):
    lenders, tensors = lax.axis_size("lender"), lax.axis_size("tensor")
    rows, depth = activations.shape
    kv_heads, slot_count, tokens, head_dim = key_pool.shape
    width = w_query.shape[1] // lenders
    out_width = w_out.shape[1]
    chunk_rows = width // head_dim * rows
    group_rows = w_query.shape[1] // head_dim // kv_heads * rows
    part_width = out_width // tensors
    f32, bf16 = jnp.float32, jnp.bfloat16
    vmem = pl.BlockSpec(memory_space=pltpu.VMEM)
    hbm = pl.BlockSpec(memory_space=pltpu.HBM)
    return pl.pallas_call(
        functools.partial(fused_kernel, lenders, tensors),
        out_shape=jax.ShapeDtypeStruct((rows // tensors, out_width), bf16),
        in_specs=[hbm] * 9,
        out_specs=vmem,
        scratch_shapes=[
            pltpu.VMEM(activations.shape, bf16),
            pltpu.VMEM(norm_gain.shape, bf16),
            pltpu.VMEM(block_list.shape, jnp.int32),
            pltpu.VMEM(block_slot_table.shape, jnp.int32),
            pltpu.VMEM(kept_len.shape[::-1], jnp.int32),
            pltpu.VMEM((lenders, depth, width), bf16),
            pltpu.VMEM((lenders, width, out_width), bf16),
            pltpu.VMEM(key_pool.shape, bf16),
            pltpu.VMEM(key_pool.shape, bf16),
            pltpu.VMEM((lenders, rows, width + LANES), f32),
            pltpu.VMEM((lenders, rows, width + LANES), f32),
            pltpu.VMEM((lenders, chunk_rows, head_dim), bf16),
            pltpu.VMEM((kv_heads, rows, slot_count * tokens), f32),
            pltpu.VMEM((kv_heads, group_rows, slot_count * tokens), f32),
            pltpu.VMEM((lenders, chunk_rows + SUBLANES, head_dim), f32),
            pltpu.VMEM((lenders, chunk_rows + SUBLANES, head_dim), f32),
            pltpu.VMEM((lenders, chunk_rows, head_dim), bf16),
            pltpu.VMEM((tensors, rows, part_width), f32),
            pltpu.VMEM((tensors, rows, part_width), f32),
            pltpu.SemaphoreType.DMA((5,)),
            pltpu.SemaphoreType.DMA((lenders,)),
            pltpu.SemaphoreType.DMA((lenders,)),
            pltpu.SemaphoreType.DMA((2,)),
            pltpu.SemaphoreType.DMA((4, lenders)),
            pltpu.SemaphoreType.DMA((4, lenders)),
            pltpu.SemaphoreType.DMA((tensors,)),
            pltpu.SemaphoreType.DMA((tensors,)),
        ],
        compiler_params=pltpu.CompilerParams(
            collective_id=0, has_side_effects=True, vmem_limit_bytes=48 * 2**20
        ),
        name="decode_attention",
    )(
        *(
            pltpu.with_memory_space_constraint(array, pltpu.HBM)
            for array in (
                activations,
                norm_gain,
                block_list,
                block_slot_table,
                kept_len.T,
                w_query,
                w_out,
                key_pool,
                value_block_store,
            )
        )
    )


def per_device(*arrays):
    activations, _, w_query, w_out, key_pool = arrays[:5]
    lenders, tensors = lax.axis_size("lender"), lax.axis_size("tensor")
    rows = activations.shape[0]
    kv_heads, slot_count, tokens, head_dim = key_pool.shape
    columns, out_width = w_query.shape[1], w_out.shape[1]
    width = columns // lenders
    fits = (
        rows == SUBLANES
        and head_dim == LANES
        and tokens == LANES
        and columns % (lenders * head_dim) == 0
        and columns // kv_heads % max(width, 1) == 0
        and width * rows % (2 * SUBLANES * head_dim) == 0
        and width * rows <= LANES * head_dim
        and rows % tensors == 0
        and out_width % (tensors * LANES) == 0
        and slot_count * tokens % 512 == 0
    )
    return (fused if fits else separate_ops)(*arrays)


def solution(mesh):
    in_specs = (
        P("group", "lender"),
        P("lender"),
        P("lender", "tensor"),
        P("tensor", "lender"),
        P("tensor", ("group", "lender"), None, None),
        P("tensor", ("group", "lender"), None, None),
        P("group", "tensor", None),
        P("tensor", "group"),
        P("group", "tensor"),
    )
    out_specs = P(("group", "tensor"), "lender")
    return jax.shard_map(
        per_device, mesh=mesh, in_specs=in_specs, out_specs=out_specs, check_vma=False
    )
```

profile of v0, /device:TPU:0, one launch (start us, length us, event | category | flops | bytes accessed | tf_op | source)
XLA Modules:
  0.0 28.3 jit_solution(1825571910697012274)
XLA Ops:
  0.0 27.7 %decode_attention.1 = bf16[2,2048]{1,0:T(2,128)(2,1)S(1)} custom-call(bf16[8,2048]{1,0:T(8,128)(2,1)} %act_hbm.1, bf16[2048]{0:T(1024)(128)(2,1)} %gain_hbm.1, s32[8,2,16]{2,1,0:T(2,128)} %list_hbm.1, s32[2,128]{1,0:T(2,128)} %table_hbm.1, s32[2,8]{1,0:T(2,128)} %bitcast.1, bf16[2048,2048]{1,0:T(8,128)(2,1)} %wq_hbm.1, bf16[2048,2048]{1,0:T(8,128)(2,1)} %wo_hbm.1, ...), custom_call_target="tpu_custom_call" | custom-call | tf_op jit(solution)/shard_map/decode_attention/pallas_call | solution.py:454
  27.7 0.6 %copy.11 = bf16[2,2048]{1,0:T(2,128)(2,1)} copy(bf16[2,2048]{1,0:T(2,128)(2,1)S(1)} %decode_attention.1) | data formatting | bytes 16384
where the time goes:
time: 28.4 us; the launch traced here: 28.3 us
  Pallas kernels  27.7 us (98%)
  local copies, waits for them, and re-layouts  0.6 us (2%)
    pallas_call x1, Pallas kernels, fused(): pl.pallas_call(functools.partial(fused_kernel, lenders, tensors), out_sha...  27.7 us
    unnamed x1, local copies, waits for them, and re-layouts  0.6 us

commit v1 on v0

--- a/solution.py
+++ b/solution.py
@@ -110,6 +110,7 @@
 
 
 def fused_kernel(
+    groups,
     lenders,
     tensors,
     act_hbm,
@@ -147,9 +148,12 @@
     kv_sem,
     lender_send,
     lender_recv,
+    att_send,
+    att_recv,
     tensor_send,
     tensor_recv,
 ):
+    part = lax.axis_index("group")
     me = lax.axis_index("lender")
     mine = lax.axis_index("tensor")
     rows = act_ref.shape[0]
@@ -158,6 +162,7 @@
     chunk_heads = width // head_dim
     chunk_rows = chunk_heads * rows
     group = wo.shape[0] * chunk_heads // kv_heads
+    share = wo.shape[2]
     chunks_per_kv = group // chunk_heads
     kept_most = list_ref.shape[2]
     f32, bf16 = jnp.float32, jnp.bfloat16
@@ -190,8 +195,9 @@
     for offset in range(lenders):
         source = lender_at(lenders - offset)
         lines = pl.ds(pl.multiple_of(source * width, width), width)
+        columns = pl.ds(pl.multiple_of(part * share, share), share)
         wo_copies.append(
-            pltpu.make_async_copy(wo_hbm.at[lines], wo.at[offset], wo_sem.at[offset])
+            pltpu.make_async_copy(wo_hbm.at[lines, columns], wo.at[offset], wo_sem.at[offset])
         )
     for copy in small_copies[:2]:
         copy.start()
@@ -199,17 +205,24 @@
         copy.start()
 
     barrier = pltpu.get_barrier_semaphore()
-    for offset in range(1, lenders):
-        pl.semaphore_signal(
-            barrier, inc=1, device_id={"lender": lender_at(offset)}, device_id_type=MESH
-        )
-    for offset in range(1, tensors):
-        pl.semaphore_signal(
-            barrier,
-            inc=1,
-            device_id={"tensor": lax.rem(mine + offset, tensors)},
-            device_id_type=MESH,
-        )
+    def group_at(step):
+        return lax.rem(part + step, groups)
+
+    def tensor_at(offset):
+        return lax.rem(mine + offset, tensors)
+
+    greeted = [
+        {"group": group_at(step), "lender": lender_at(offset)}
+        for step in range(groups)
+        for offset in range(lenders)
+        if (step, offset) != (0, 0)
+    ] + [
+        {"group": group_at(step), "tensor": tensor_at(offset)}
+        for step in range(groups)
+        for offset in range(1, tensors)
+    ]
+    for device in greeted:
+        pl.semaphore_signal(barrier, inc=1, device_id=device, device_id_type=MESH)
 
     def to_lender(stage, offset, src, dst):
         return pltpu.make_async_remote_copy(
@@ -246,7 +259,7 @@
         q_send[offset, :, :width] = partial
         q_send[offset, :, width:] = jnp.broadcast_to(squares, (rows, LANES))
         if at == 0:
-            pl.semaphore_wait(barrier, lenders + tensors - 2)
+            pl.semaphore_wait(barrier, len(greeted))
         copy = to_lender(0, offset, q_send.at[offset], q_recv.at[offset])
         copy.start()
         started.append(copy)
@@ -372,59 +385,86 @@
         factor = jnp.exp(bests[offset] - highest)
         home_total = home_total + totals[offset] * factor
         home_value = home_value + part_recv[offset, :chunk_rows, :] * factor
-    att_all[me] = (home_value / home_total).astype(bf16)
+    att_all[part, me] = (home_value / home_total).astype(bf16)
     att_copies = {}
-    for offset in far_first:
-        copy = to_lender(3, offset, att_all.at[me], att_all.at[me])
-        copy.start()
-        att_copies[offset] = copy
+    for offset in far_first + [0]:
+        for step in range(groups):
+            if (step, offset) == (0, 0):
+                continue
+            copy = pltpu.make_async_remote_copy(
+                src_ref=att_all.at[part, me],
+                dst_ref=att_all.at[part, me],
+                send_sem=att_send.at[step, offset],
+                recv_sem=att_recv.at[step, offset],
+                device_id={"group": group_at(step), "lender": lender_at(offset)},
+                device_id_type=MESH,
+            )
+            copy.start()
+            att_copies[step, offset] = copy
     started += att_copies.values()
 
     product = None
     for offset in range(lenders):
         wo_copies[offset].wait()
-        if offset > 0:
-            att_copies[offset].wait_recv()
-        chunk = att_all[lender_at(lenders - offset)].astype(f32)
-        chunk = jnp.concatenate(
-            [chunk[j * rows : (j + 1) * rows] for j in range(chunk_heads)], axis=1
-        ).astype(bf16)
+        for step in range(groups):
+            if (step, offset) != (0, 0):
+                att_copies[step, offset].wait_recv()
+        source = lender_at(lenders - offset)
+        chunks = []
+        for g in range(groups):
+            chunk = att_all[g, source].astype(f32)
+            chunks.append(
+                jnp.concatenate(
+                    [chunk[j * rows : (j + 1) * rows] for j in range(chunk_heads)], axis=1
+                )
+            )
+        chunk = jnp.concatenate(chunks, axis=0).astype(bf16)
         term = jnp.dot(chunk, wo[offset], preferred_element_type=f32)
         product = term if product is None else product + term
 
     home_rows = rows // tensors
-    part_width = product.shape[1] // tensors
+    part_width = share // tensors
     line_block = lax.broadcasted_iota(jnp.int32, (rows, part_width), 0) // home_rows
-    for d in range(tensors):
-        packed = jnp.zeros((rows, part_width), f32)
+    for g in range(groups):
+        for d in range(tensors):
+            packed = jnp.zeros((rows, part_width), f32)
+            for c in range(tensors):
+                piece = product[
+                    g * rows : (g + 1) * rows, c * part_width : (c + 1) * part_width
+                ]
+                shift = (c - d) * home_rows % rows
+                if shift:
+                    piece = pltpu.roll(piece, shift, 0)
+                packed = jnp.where(line_block == c, piece, packed)
+            sum_send[g, d] = packed
+    sum_copies = []
+    for step in range(groups):
+        for offset in range(tensors):
+            if (step, offset) == (0, 0):
+                continue
+            copy = pltpu.make_async_remote_copy(
+                src_ref=sum_send.at[group_at(step), tensor_at(offset)],
+                dst_ref=sum_recv.at[part, offset],
+                send_sem=tensor_send.at[step, offset],
+                recv_sem=tensor_recv.at[step, offset],
+                device_id={"group": group_at(step), "tensor": tensor_at(offset)},
+                device_id_type=MESH,
+            )
+            copy.start()
+            sum_copies.append(copy)
+    started += sum_copies
+    sum_recv[part, 0] = sum_send[part, mine]
+    for copy in sum_copies:
+        copy.wait_recv()
+    for g in range(groups):
+        result = sum_recv[g, 0]
+        for offset in range(1, tensors):
+            result = result + sum_recv[g, offset]
         for c in range(tensors):
-            piece = product[:, c * part_width : (c + 1) * part_width]
-            shift = (c - d) * home_rows % rows
-            if shift:
-                piece = pltpu.roll(piece, shift, 0)
-            packed = jnp.where(line_block == c, piece, packed)
-        sum_send[d] = packed
-    for offset in range(1, tensors):
-        target = lax.rem(mine + offset, tensors)
-        copy = pltpu.make_async_remote_copy(
-            src_ref=sum_send.at[target],
-            dst_ref=sum_recv.at[offset],
-            send_sem=tensor_send.at[offset],
-            recv_sem=tensor_recv.at[offset],
-            device_id={"tensor": target},
-            device_id_type=MESH,
-        )
-        copy.start()
-        started.append(copy)
-    result = sum_send[mine]
-    for copy in started[1 - tensors :] if tensors > 1 else []:
-        copy.wait_recv()
-    for offset in range(1, tensors):
-        result = result + sum_recv[offset]
-    for c in range(tensors):
-        out_ref[:, c * part_width : (c + 1) * part_width] = result[
-            c * home_rows : (c + 1) * home_rows
-        ].astype(out_ref.dtype)
+            at = g * share + c * part_width
+            out_ref[:, at : at + part_width] = result[
+                c * home_rows : (c + 1) * home_rows
+            ].astype(out_ref.dtype)
     for copy in started:
         copy.wait_send()
 
@@ -440,6 +480,7 @@
     block_slot_table,
     kept_len,
 ):
+    groups = lax.axis_size("group")
     lenders, tensors = lax.axis_size("lender"), lax.axis_size("tensor")
     rows, depth = activations.shape
     kv_heads, slot_count, tokens, head_dim = key_pool.shape
@@ -447,12 +488,13 @@
     out_width = w_out.shape[1]
     chunk_rows = width // head_dim * rows
     group_rows = w_query.shape[1] // head_dim // kv_heads * rows
-    part_width = out_width // tensors
+    share = out_width // groups
+    part_width = share // tensors
     f32, bf16 = jnp.float32, jnp.bfloat16
     vmem = pl.BlockSpec(memory_space=pltpu.VMEM)
     hbm = pl.BlockSpec(memory_space=pltpu.HBM)
     return pl.pallas_call(
-        functools.partial(fused_kernel, lenders, tensors),
+        functools.partial(fused_kernel, groups, lenders, tensors),
         out_shape=jax.ShapeDtypeStruct((rows // tensors, out_width), bf16),
         in_specs=[hbm] * 9,
         out_specs=vmem,
@@ -463,7 +505,7 @@
             pltpu.VMEM(block_slot_table.shape, jnp.int32),
             pltpu.VMEM(kept_len.shape[::-1], jnp.int32),
             pltpu.VMEM((lenders, depth, width), bf16),
-            pltpu.VMEM((lenders, width, out_width), bf16),
+            pltpu.VMEM((lenders, width, share), bf16),
             pltpu.VMEM(key_pool.shape, bf16),
             pltpu.VMEM(key_pool.shape, bf16),
             pltpu.VMEM((lenders, rows, width + LANES), f32),
@@ -473,17 +515,19 @@
             pltpu.VMEM((kv_heads, group_rows, slot_count * tokens), f32),
             pltpu.VMEM((lenders, chunk_rows + SUBLANES, head_dim), f32),
             pltpu.VMEM((lenders, chunk_rows + SUBLANES, head_dim), f32),
-            pltpu.VMEM((lenders, chunk_rows, head_dim), bf16),
-            pltpu.VMEM((tensors, rows, part_width), f32),
-            pltpu.VMEM((tensors, rows, part_width), f32),
+            pltpu.VMEM((groups, lenders, chunk_rows, head_dim), bf16),
+            pltpu.VMEM((groups, tensors, rows, part_width), f32),
+            pltpu.VMEM((groups, tensors, rows, part_width), f32),
             pltpu.SemaphoreType.DMA((5,)),
             pltpu.SemaphoreType.DMA((lenders,)),
             pltpu.SemaphoreType.DMA((lenders,)),
             pltpu.SemaphoreType.DMA((2,)),
-            pltpu.SemaphoreType.DMA((4, lenders)),
-            pltpu.SemaphoreType.DMA((4, lenders)),
-            pltpu.SemaphoreType.DMA((tensors,)),
-            pltpu.SemaphoreType.DMA((tensors,)),
+            pltpu.SemaphoreType.DMA((3, lenders)),
+            pltpu.SemaphoreType.DMA((3, lenders)),
+            pltpu.SemaphoreType.DMA((groups, lenders)),
+            pltpu.SemaphoreType.DMA((groups, lenders)),
+            pltpu.SemaphoreType.DMA((groups, tensors)),
+            pltpu.SemaphoreType.DMA((groups, tensors)),
         ],
         compiler_params=pltpu.CompilerParams(
             collective_id=0, has_side_effects=True, vmem_limit_bytes=48 * 2**20
@@ -523,7 +567,7 @@
         and width * rows % (2 * SUBLANES * head_dim) == 0
         and width * rows <= LANES * head_dim
         and rows % tensors == 0
-        and out_width % (tensors * LANES) == 0
+        and out_width % (lax.axis_size("group") * tensors * LANES) == 0
         and slot_count * tokens % 512 == 0
     )
     return (fused if fits else separate_ops)(*arrays)

time: 28.4 us -> 29.7 us (1.046)
  Pallas kernels: 27.7 us -> 29 us
    pallas_call x1, Pallas kernels: 27.7 us -> 29 us  [fused(): pl.pallas_call(functools.partial(fused_kernel, groups, lenders, tensors),...]
where the time goes in v1:
time: 29.7 us; the launch traced here: 29.6 us
  Pallas kernels  29 us (98%)
  local copies, waits for them, and re-layouts  0.6 us (2%)
    pallas_call x1, Pallas kernels, fused(): pl.pallas_call(functools.partial(fused_kernel, groups, lenders, tensors),...  29 us
    unnamed x1, local copies, waits for them, and re-layouts  0.6 us

profile of v1, /device:TPU:0, one launch (start us, length us, event | category | flops | bytes accessed | tf_op | source)
XLA Modules:
  0.0 29.6 jit_solution(1671529581121500889)
XLA Ops:
  0.0 29.0 %decode_attention.1 = bf16[2,2048]{1,0:T(2,128)(2,1)S(1)} custom-call(bf16[8,2048]{1,0:T(8,128)(2,1)} %act_hbm.1, bf16[2048]{0:T(1024)(128)(2,1)} %gain_hbm.1, s32[8,2,16]{2,1,0:T(2,128)} %list_hbm.1, s32[2,128]{1,0:T(2,128)} %table_hbm.1, s32[2,8]{1,0:T(2,128)} %bitcast.1, bf16[2048,2048]{1,0:T(8,128)(2,1)} %wq_hbm.1, bf16[2048,2048]{1,0:T(8,128)(2,1)} %wo_hbm.1, ...), custom_call_target="tpu_custom_call" | custom-call | tf_op jit(solution)/shard_map/decode_attention/pallas_call | solution.py:496
  29.0 0.6 %copy.11 = bf16[2,2048]{1,0:T(2,128)(2,1)} copy(bf16[2,2048]{1,0:T(2,128)(2,1)S(1)} %decode_attention.1) | data formatting | bytes 16384

commit v2 on v0

--- a/solution.py
+++ b/solution.py
@@ -234,14 +234,11 @@
         if at == 0:
             for copy in small_copies[2:]:
                 copy.start()
-            key_copy.start()
-            value_copy.start()
-        if at == min(1, lenders - 1):
-            for copy in wo_copies:
-                copy.start()
         partial = jnp.dot(scaled, wq[offset], preferred_element_type=f32)
         if offset == 0:
             own_partial = partial
+            key_copy.start()
+            value_copy.start()
             continue
         q_send[offset, :, :width] = partial
         q_send[offset, :, width:] = jnp.broadcast_to(squares, (rows, LANES))
@@ -294,6 +291,8 @@
         copy = to_lender(1, offset, q_all.at[me], q_all.at[me])
         copy.start()
         started.append(copy)
+    for copy in wo_copies:
+        copy.start()
 
     step_slots = max(1, min(slot_count, 512 // tokens))
     step = step_slots * tokens

time: 28.4 us -> 28.4 us (level)
  no operation moved by 1% of the time
where the time goes in v2:
time: 28.4 us; the launch traced here: 28.3 us
  Pallas kernels  27.7 us (98%)
  local copies, waits for them, and re-layouts  0.6 us (2%)
    pallas_call x1, Pallas kernels, fused(): pl.pallas_call(functools.partial(fused_kernel, lenders, tensors), out_sha...  27.7 us
    unnamed x1, local copies, waits for them, and re-layouts  0.6 us

profile of v2, /device:TPU:0, one launch (start us, length us, event | category | flops | bytes accessed | tf_op | source)
XLA Modules:
  0.0 28.3 jit_solution(262223190184240654)
XLA Ops:
  0.0 27.7 %decode_attention.1 = bf16[2,2048]{1,0:T(2,128)(2,1)S(1)} custom-call(bf16[8,2048]{1,0:T(8,128)(2,1)} %act_hbm.1, bf16[2048]{0:T(1024)(128)(2,1)} %gain_hbm.1, s32[8,2,16]{2,1,0:T(2,128)} %list_hbm.1, s32[2,128]{1,0:T(2,128)} %table_hbm.1, s32[2,8]{1,0:T(2,128)} %bitcast.1, bf16[2048,2048]{1,0:T(8,128)(2,1)} %wq_hbm.1, bf16[2048,2048]{1,0:T(8,128)(2,1)} %wo_hbm.1, ...), custom_call_target="tpu_custom_call" | custom-call | tf_op jit(solution)/shard_map/decode_attention/pallas_call | solution.py:453
  27.7 0.6 %copy.11 = bf16[2,2048]{1,0:T(2,128)(2,1)} copy(bf16[2,2048]{1,0:T(2,128)(2,1)S(1)} %decode_attention.1) | data formatting | bytes 16384

commit v3 on v0

--- a/solution.py
+++ b/solution.py
@@ -302,18 +302,14 @@
         jnp.int32, (chunk_rows, LANES), 1
     )
     first_line = lax.broadcasted_iota(jnp.int32, (SUBLANES, LANES), 0) == 0
+    key_copy.wait()
+    for copy in started[-len(far_first) :] if far_first else []:
+        copy.wait_recv()
+    high = []
     for h in range(kv_heads):
-        chunks = range(h * chunks_per_kv, (h + 1) * chunks_per_kv)
-        for source in chunks:
-
-            @pl.when(me != source)
-            def _():
-                offset = lax.rem(me - source + lenders, lenders)
-                to_lender(1, offset, q_all.at[source], q_all.at[source]).wait_recv()
-
-        if h == 0:
-            key_copy.wait()
-        queries = q_all[chunks.start : chunks.stop].reshape(group * rows, head_dim)
+        queries = q_all[h * chunks_per_kv : (h + 1) * chunks_per_kv].reshape(
+            group * rows, head_dim
+        )
         running = None
         for c in range(steps):
             block = keys[h, c * step_slots : (c + 1) * step_slots].reshape(step, head_dim)
@@ -326,9 +322,11 @@
             for t in range(0, step, LANES):
                 piece = found[:, t : t + LANES]
                 running = piece if running is None else jnp.maximum(running, piece)
-        best = jnp.max(running, axis=1, keepdims=True)
-        if h == 0:
-            value_copy.wait()
+        high.append(jnp.max(running, axis=1, keepdims=True))
+    value_copy.wait()
+    for h in range(kv_heads):
+        chunks = range(h * chunks_per_kv, (h + 1) * chunks_per_kv)
+        best = high[h]
         total = None
         gathered = jnp.zeros((group * rows, head_dim), f32)
         for c in range(steps):

time: 28.4 us -> 28.5 us (level)
  no operation moved by 1% of the time
where the time goes in v3:
time: 28.5 us; the launch traced here: 28.4 us
  Pallas kernels  27.8 us (98%)
  local copies, waits for them, and re-layouts  0.6 us (2%)
    pallas_call x1, Pallas kernels, fused(): pl.pallas_call(functools.partial(fused_kernel, lenders, tensors), out_sha...  27.8 us
    unnamed x1, local copies, waits for them, and re-layouts  0.6 us

profile of v3, /device:TPU:0, one launch (start us, length us, event | category | flops | bytes accessed | tf_op | source)
XLA Modules:
  0.0 28.4 jit_solution(12267112322802629332)
XLA Ops:
  0.0 27.8 %decode_attention.1 = bf16[2,2048]{1,0:T(2,128)(2,1)S(1)} custom-call(bf16[8,2048]{1,0:T(8,128)(2,1)} %act_hbm.1, bf16[2048]{0:T(1024)(128)(2,1)} %gain_hbm.1, s32[8,2,16]{2,1,0:T(2,128)} %list_hbm.1, s32[2,128]{1,0:T(2,128)} %table_hbm.1, s32[2,8]{1,0:T(2,128)} %bitcast.1, bf16[2048,2048]{1,0:T(8,128)(2,1)} %wq_hbm.1, bf16[2048,2048]{1,0:T(8,128)(2,1)} %wo_hbm.1, ...), custom_call_target="tpu_custom_call" | custom-call | tf_op jit(solution)/shard_map/decode_attention/pallas_call | solution.py:452
  27.8 0.6 %copy.11 = bf16[2,2048]{1,0:T(2,128)(2,1)} copy(bf16[2,2048]{1,0:T(2,128)(2,1)S(1)} %decode_attention.1) | data formatting | bytes 16384
